TPU v7x, 32 devices: a whole 2x2x4 slice. The times are simulated.
32 devices in a mesh: groups: 2 (over y), pair: 8 (over z, x), aux: 2 (over core).
Axes of the slice: x: 2, y: 2, z: 4, core: 2. Of those that a mesh axis runs over, the one named last changes fastest.
Arguments:
- factors: float32 [8192, 2048], P(('groups', 'pair', 'aux')), parts along dimension 0, may hold values from -0.6 to 0.6
- occupied_energy: float32 [256], P('groups'), parts along dimension 0, may hold values from -3 to -0.4
- virtual_energy: float32 [4096], P('groups'), parts along dimension 0, may hold values from 0.2 to 4
- batch_orbitals: int32 [2], P('groups'), parts along dimension 0, may hold values from 0 to 127, as said below
- panel_order: int32 [32], P('groups'), parts along dimension 0, may hold values from 0 to 31, as said below
Outputs:
- density: float32 [8192, 2048], P(('groups', 'pair', 'aux')), parts along dimension 0
There are 2 independent parts, one for each index of `groups`. A program takes and returns all parts, laid end to end along the dimension named above; each array names one. Nothing has to cross between parts.
Inputs may be any that keep to these rules, and one draw needn't show every extreme that they name: `batch_orbitals`: 1 distinct occupied orbitals. `panel_order`: 16 distinct panel numbers.
All inputs are finite; a program needn't handle non-finite values.
Results may differ from a plain program's by a relative error of at most 0.0001.
Values sent between devices are 32-bit elements; how exact they have to be, the bound alone decides.
A program may use at most 64 MiB of HBM per device.

v0:
```python
import jax
import jax.numpy as jnp
from jax import lax
from jax.sharding import PartitionSpec as P

PANEL = 64


os_scale = 1.3


def spread(block, axis, source):
    block = jnp.where(lax.axis_index(axis) == source, block, jnp.zeros_like(block))
    return lax.psum(block, axis)


def column_energies(columns, batch_energy, virtual_energy):
    nvir = virtual_energy.shape[0]
    nbatch = batch_energy.shape[0]
    orbital = columns // nvir
    virtual = columns % nvir
    occ_part = jnp.sum(
        jnp.where(
            orbital[:, None] == jnp.arange(nbatch, dtype=jnp.int32)[None, :],
            batch_energy[None, :],
            0.0,
        ),
        axis=1,
    )
    vir_part = jnp.sum(
        jnp.where(
            virtual[:, None] == jnp.arange(nvir, dtype=jnp.int32)[None, :],
            virtual_energy[None, :],
            0.0,
        ),
        axis=1,
    )
    return vir_part - occ_part


def batch_energies(occupied_energy, batch_orbitals):
    noccupied = occupied_energy.shape[0]
    return jnp.sum(
        jnp.where(
            batch_orbitals[:, None] == jnp.arange(noccupied, dtype=jnp.int32)[None, :],
            occupied_energy[None, :],
            0.0,
        ),
        axis=1,
    )


def by_columns(factors, occupied_energy, virtual_energy, batch_orbitals, panel_order):
    pair_count = lax.axis_size("pair")
    total_columns = factors.shape[1]
    col_local = total_columns // pair_count
    per_owner = col_local // PANEL
    working = lax.all_to_all(factors, "pair", split_axis=1, concat_axis=0, tiled=True)
    batch_energy = batch_energies(occupied_energy, batch_orbitals)
    own_columns = lax.axis_index("pair") * col_local + jnp.arange(col_local, dtype=jnp.int32)
    own_energy = column_energies(own_columns, batch_energy, virtual_energy)

    def one_panel(position, density):
        number = panel_order[position]
        owner_index = number // per_owner
        panel_slab = lax.dynamic_slice_in_dim(working, number % per_owner * PANEL, PANEL, 1)
        panel_block = spread(panel_slab, "pair", owner_index)
        panel_energy = column_energies(
            number * PANEL + jnp.arange(PANEL, dtype=jnp.int32), batch_energy, virtual_energy
        )
        partial_ints = lax.dot_general(
            panel_block,
            working,
            (((0,), (0,)), ((), ())),
            precision=lax.Precision.HIGHEST,
            preferred_element_type=jnp.float32,
        )
        integrals = lax.psum(partial_ints, "aux")
        amplitudes = os_scale * integrals / (own_energy[None, :] + panel_energy[:, None])
        return density + jnp.dot(
            panel_block,
            amplitudes,
            precision=lax.Precision.HIGHEST,
            preferred_element_type=jnp.float32,
        )

    density = lax.fori_loop(
        0, panel_order.shape[0], one_panel, jnp.zeros(working.shape, jnp.float32)
    )
    return lax.all_to_all(density, "pair", split_axis=0, concat_axis=1, tiled=True)


def by_rows(factors, occupied_energy, virtual_energy, batch_orbitals, panel_order):
    total = factors.shape[1]
    batch_energy = batch_energies(occupied_energy, batch_orbitals)
    nvir = virtual_energy.shape[0]
    energy = (virtual_energy[None, :] - batch_energy[:, None]).reshape(-1)
    panels = jnp.concatenate(
        [
            lax.dynamic_slice_in_dim(factors, panel_order[k] * PANEL, PANEL, 1)
            for k in range(panel_order.shape[0])
        ],
        axis=1,
    )
    chosen = jnp.concatenate(
        [
            lax.dynamic_slice_in_dim(energy, panel_order[k] * PANEL, PANEL, 0)
            for k in range(panel_order.shape[0])
        ]
    )
    partial = lax.dot_general(
        panels,
        factors,
        (((0,), (0,)), ((), ())),
        precision=lax.Precision.HIGH,
        preferred_element_type=jnp.float32,
    )
    mine = lax.psum_scatter(partial, ("pair", "aux"), scatter_dimension=0, tiled=True)
    rank = lax.axis_index("pair") * lax.axis_size("aux") + lax.axis_index("aux")
    my_energy = lax.dynamic_slice_in_dim(chosen, rank * mine.shape[0], mine.shape[0], 0)
    mine = os_scale * mine / (energy[None, :] + my_energy[:, None])
    amplitudes = lax.all_gather(mine, ("pair", "aux"), axis=0, tiled=True)
    return jnp.dot(
        panels, amplitudes, precision=lax.Precision.HIGH, preferred_element_type=jnp.float32
    )


def on_device(factors, occupied_energy, virtual_energy, batch_orbitals, panel_order):
    window = panel_order.shape[0] * PANEL
    fits = 4 * window * factors.shape[1] <= 8 * 1024 * 1024
    plan = by_rows if fits else by_columns
    return plan(factors, occupied_energy, virtual_energy, batch_orbitals, panel_order)


def solution(mesh):
    in_specs = (
        P(("groups", "pair", "aux"), None),
        P("groups"),
        P("groups"),
        P("groups"),
        P("groups"),
    )
    out_specs = P(("groups", "pair", "aux"), None)
    return jax.shard_map(
        on_device, mesh=mesh, in_specs=in_specs, out_specs=out_specs, check_vma=False
    )
```

profile of v0, /device:TPU:1, one launch (start us, length us, event | category | flops | bytes accessed | tf_op | source)
XLA Modules:
  0.0 228.6 jit_solution(1374346407316018232)
XLA Ops:
  6.5 0.0 reduce-scatter.2.cloned.1.call-start
  6.5 2.0 fusion.2
  18.7 3.4 %constant_dynamic-slice_fusion = (f32[256,64]{1,0:T(8,128)S(1)}, f32[256,64]{1,0:T(8,128)S(1)}, f32[256,64]{1,0:T(8,128)S(1)}, f32[256,64]{1,0:T(8,128)}, f32[25...) fusion(f32[256,2048]{1,0:T(8,128)} %param.5, ...), kind=kLoop, calls=%fused_computation.2 | loop fusion | bytes 2097216 | tf_op jit(solution)/shard_map/dynamic_slice | solution.py:100
  22.1 0.0 copy-start
  22.1 1.9 concatenate.6
  24.0 0.3 copy-done
  24.3 5.8 %fusion.3 = f32[1024,2048]{1,0:T(8,128)} fusion(f32[256,1024]{1,0:T(8,128)S(1)} %concatenate.6, f32[256,2048]{1,0:T(8,128)S(1)} %copy-done), kind=kOutput, calls=%fused_computation.22 | convolution fusion | flops 3221225472 | bytes 11534336 | tf_op jit(solution)/shard_map/dot_general | solution.py:111
  30.1 0.0 copy-start.2
  30.1 0.0 copy-start.1
  30.1 0.0 reduce-scatter.2.cloned.1.call-update
  30.1 0.0 all-gather.2.cloned.1.call-start
  30.8 0.0 copy-done.2
  30.8 0.6 fusion
  31.5 0.0 copy-done.1
  31.5 0.6 broadcast_subtract_fusion
  32.1 0.2 fusion.1
  32.3 0.1 concatenate.7
  32.3 0.1 dynamic_slice.131
  32.4 104.6 %reduce-scatter.2.cloned.1.call-done = f32[64,2048]{1,0:T(8,128)} async-done(((f32[1024,2048]{1,0:T(8,128)}), f32[64,2048]{1,0:T(8,128)}) %reduce-scatter.2.cloned.1.call-update) | async-done | bytes 524304 | tf_op jit(solution)/shard_map/reduce_scatter | solution.py:118
  137.0 2.0 add_divide_fusion
  139.0 0.0 all-gather.2.cloned.1.call-update
  139.0 75.2 %all-gather.2.cloned.1.call-done = f32[1024,2048]{1,0:T(8,128)} async-done(((f32[64,2048]{1,0:T(8,128)}), f32[1024,2048]{1,0:T(8,128)}) %all-gather.2.cloned.1.call-update) | async-done | bytes 8388624 | tf_op jit(solution)/shard_map/all_gather | solution.py:122
  214.2 7.6 %fusion.4 = f32[256,2048]{1,0:T(8,128)} fusion(f32[256,1024]{1,0:T(8,128)S(1)} %concatenate.6, f32[1024,2048]{1,0:T(8,128)} %all-gather.2.cloned.1.call-done), kind=kOutput, calls=%fused_computation.23 | convolution fusion | flops 3221225472 | bytes 11534336 | tf_op jit(solution)/shard_map/dot_general | solution.py:123
Async XLA Ops:
  6.5 130.4 %reduce-scatter.2.cloned.1.call-start = ((), (), s32[]{:S(2)}) async-start(), calls=%async_computation.1 | async-start | bytes 8912896 | tf_op jit(solution)/shard_map/reduce_scatter | solution.py:118
  22.1 2.2 copy-start
  30.1 0.7 copy-start.2
  30.1 1.4 copy-start.1
  30.1 184.1 %all-gather.2.cloned.1.call-start = ((), (), s32[]{:S(2)}) async-start(), calls=%async_computation.2 | async-start | bytes 8912896 | tf_op jit(solution)/shard_map/all_gather | solution.py:122
Sparse Core Ops, SparseCore 0:
  30.2 106.6 reduce-scatter.1
  139.1 75.0 all-gather.1
where the time goes:
time: 229 us
  waiting for transfers between devices  180 us (79%)
  between operations  24.3 us (11%)
  matrix products  13.4 us (6%)
  local copies, waits for them, and re-layouts  7.91 us (3%)
  other arithmetic  3.25 us (1%)
    reduce_scatter x1, waiting for transfers between devices, by_rows(): lax.psum_scatter(partial, ('pair', 'aux'), scatter_dimension=0, tiled=True)  105 us
    all_gather x1, waiting for transfers between devices, by_rows(): amplitudes = lax.all_gather(mine, ('pair', 'aux'), axis=0, tiled=True)  75.2 us
    dot_general x1, matrix products, by_rows(): jnp.dot(panels, amplitudes, precision=lax.Precision.HIGH, preferred_eleme...  7.56 us
    dot_general x1, matrix products, by_rows(): lax.dot_general(panels, factors, (((0,), (0,)), ((), ())), precision=lax....  5.8 us
  transfers between devices with their start and end apart: 2, of which 2 were waited for; matrix products, arithmetic and copies ran while one was open for 1% of the time, Pallas kernels for 0%

commit v1 on v0

--- a/solution.py
+++ b/solution.py
@@ -1,6 +1,10 @@
+import functools
+
 import jax
 import jax.numpy as jnp
 from jax import lax
+from jax.experimental import pallas as pl
+from jax.experimental.pallas import tpu as pltpu
 from jax.sharding import PartitionSpec as P
 
 PANEL = 64
@@ -90,10 +94,238 @@
     return lax.all_to_all(density, "pair", split_axis=0, concat_axis=1, tiled=True)
 
 
+SUB = 2
+
+
+def split(x):
+    high = x.astype(jnp.bfloat16)
+    return high, (x - high.astype(jnp.float32)).astype(jnp.bfloat16)
+
+
+def dot3(a_high, a_low, b_high, b_low):
+    dot = functools.partial(jnp.dot, preferred_element_type=jnp.float32)
+    return dot(a_high, b_high) + dot(a_high, b_low) + dot(a_low, b_high)
+
+
+def ring_place(pair, n):
+    side = pair % 2
+    level = pair // 2
+    return level + side * (n - 1 - 2 * level)
+
+
+def ring_pair(place, n):
+    side = place // (n // 2)
+    level = place + side * (n - 1 - 2 * place)
+    return 2 * level + side
+
+
+def ring_kernel(
+    n, b_ref, p_ref, col_ref, row_ref, out_ref,
+    sib_b, sib_p, pt_high, pt_low, p_high, p_low, part, buf, amp,
+    sibp_send, sibp_recv, sibb_send, sibb_recv,
+    red_send, red_recv, gat_send, gat_recv, siba_send, siba_recv,
+):
+    depth, total = b_ref.shape
+    window = p_ref.shape[1]
+    width = total // n
+    half = window // 2
+    quarter = half // 2
+    rows = quarter // SUB
+    core = lax.axis_index("aux")
+    place = ring_place(lax.axis_index("pair"), n)
+
+    def neighbour(d):
+        return {"pair": ring_pair((place + n + 1 - 2 * d) % n, n)}
+
+    sibling = {"aux": 1 - core}
+
+    def columns(q):
+        return pl.ds(pl.multiple_of(q * width, width), width)
+
+    def shard(d, step):
+        return (place + n * n + (2 * d - 1) * step) % n
+
+    def sib_p_copy():
+        return pltpu.make_async_remote_copy(
+            p_ref.at[:, pl.ds(pl.multiple_of((1 - core) * half, half), half)], sib_p,
+            sibp_send, sibp_recv, device_id=sibling, device_id_type=pl.DeviceIdType.MESH)
+
+    def sib_b_copy(q):
+        return pltpu.make_async_remote_copy(
+            b_ref.at[:, columns(q)], sib_b.at[:, columns(q)],
+            sibb_send.at[q], sibb_recv.at[q], device_id=sibling,
+            device_id_type=pl.DeviceIdType.MESH)
+
+    def sub(u):
+        return pl.ds(pl.multiple_of(u * rows, rows), rows)
+
+    def amp_rows(d, u):
+        return pl.ds(pl.multiple_of(core * half + d * quarter + u * rows, rows), rows)
+
+    def red_copy(d, s, u):
+        return pltpu.make_async_remote_copy(
+            buf.at[d, s, sub(u)], buf.at[d, s + 1, sub(u)],
+            red_send.at[d, s, u], red_recv.at[d, s, u], device_id=neighbour(d),
+            device_id_type=pl.DeviceIdType.MESH)
+
+    def gat_copy(d, s, u, q):
+        block = amp.at[amp_rows(d, u), columns(q)]
+        return pltpu.make_async_remote_copy(
+            block, block, gat_send.at[d, s, u], gat_recv.at[d, s, u],
+            device_id=neighbour(d), device_id_type=pl.DeviceIdType.MESH)
+
+    def sib_a_copy(d, t, u, q):
+        block = amp.at[amp_rows(d, u), columns(q)]
+        return pltpu.make_async_remote_copy(
+            block, block, siba_send.at[d, t, u], siba_recv.at[d, t, u],
+            device_id=sibling, device_id_type=pl.DeviceIdType.MESH)
+
+    def sib_a_arrival(d, t, u, q):
+        block = amp.at[
+            pl.ds(pl.multiple_of((1 - core) * half + d * quarter + u * rows, rows), rows),
+            columns(q)]
+        return pltpu.make_async_remote_copy(
+            block, block, siba_send.at[d, t, u], siba_recv.at[d, t, u],
+            device_id=sibling, device_id_type=pl.DeviceIdType.MESH)
+
+    barrier = pltpu.get_barrier_semaphore()
+    for other in (neighbour(0), neighbour(1), sibling):
+        pl.semaphore_signal(barrier, inc=1, device_id=other, device_id_type=pl.DeviceIdType.MESH)
+    pl.semaphore_wait(barrier, 3)
+
+    sib_p_copy().start()
+    for i in range(1, n // 2 + 1):
+        sib_b_copy(shard(0, i)).start()
+        if i < n // 2:
+            sib_b_copy(shard(1, i)).start()
+    sib_b_copy(place).start()
+
+    mine = pl.ds(pl.multiple_of(core * half, half), half)
+    high, low = split(p_ref[:, mine].T)
+    pt_high[:, :depth] = high
+    pt_low[:, :depth] = low
+    sib_p_copy().wait_recv()
+    high, low = split(sib_p[...].T)
+    pt_high[:, depth:] = high
+    pt_low[:, depth:] = low
+
+    def set_part(d, q):
+        lhs = pl.ds(pl.multiple_of(d * quarter, quarter), quarter)
+        own_high, own_low = split(b_ref[:, columns(q)])
+        sib_high, sib_low = split(sib_b[:, columns(q)])
+        part[d] = dot3(pt_high[lhs, :depth], pt_low[lhs, :depth], own_high, own_low) + dot3(
+            pt_high[lhs, depth:], pt_low[lhs, depth:], sib_high, sib_low)
+
+    @pl.loop(0, 2)
+    def _(d):
+        sib_b_copy(shard(d, 1)).wait_recv()
+        set_part(d, shard(d, 1))
+        buf[d, 0] = part[d]
+        for u in range(SUB):
+            red_copy(d, 0, u).start()
+
+    for i in range(2, n // 2 + 1):
+        sib_b_copy(shard(0, i)).wait_recv()
+        if i < n // 2:
+            sib_b_copy(shard(1, i)).wait_recv()
+    sib_b_copy(place).wait_recv()
+    high, low = split(p_ref[...])
+    p_high[...] = high
+    p_low[...] = low
+
+    @pl.loop(1, n - 1)
+    def _(s):
+        @pl.loop(0, 2)
+        def _(d):
+            set_part(d, shard(d, s + 1))
+        for u in range(SUB):
+            for d in range(2):
+                red_copy(d, s - 1, u).wait_recv()
+                buf[d, s, sub(u)] += part[d, sub(u)]
+                red_copy(d, s, u).start()
+
+    @pl.loop(0, 2)
+    def _(d):
+        set_part(d, place)
+    for u in range(SUB):
+        for d in range(2):
+            red_copy(d, n - 2, u).wait_recv()
+            integrals = buf[d, n - 1, sub(u)] + part[d, sub(u)]
+            energy = col_ref[:, columns(place)] + row_ref[amp_rows(d, u), :]
+            amp[amp_rows(d, u), columns(place)] = os_scale * integrals / energy
+            gat_copy(d, 0, u, place).start()
+            sib_a_copy(d, 0, u, place).start()
+
+    def pass_on(s, last):
+        for u in range(SUB):
+            for d in range(2):
+                q = shard(d, s + 1)
+                gat_copy(d, s, u, q).wait_recv()
+                if not last:
+                    gat_copy(d, s + 1, u, q).start()
+                sib_a_copy(d, s + 1, u, q).start()
+
+    def density(q):
+        total_sum = jnp.zeros((depth, width), jnp.float32)
+        for k in range(4):
+            span = pl.ds(k * quarter, quarter)
+            a_high, a_low = split(amp[span, columns(q)])
+            total_sum += dot3(p_high[:, span], p_low[:, span], a_high, a_low)
+        out_ref[:, columns(q)] = total_sum
+
+    def finish(d, j):
+        q = shard(d, j)
+        for u in range(SUB):
+            sib_a_arrival(d, j, u, q).wait_recv()
+            sib_a_arrival(1 - d, (n - j) % n, u, q).wait_recv()
+        density(q)
+
+    middle = n // 2
+
+    @pl.loop(0, middle)
+    def _(s):
+        pass_on(s, False)
+
+    @pl.loop(0, 2)
+    def _(i):
+        finish(0, i * middle)
+
+    @pl.loop(middle, n - 2)
+    def _(s):
+        pass_on(s, False)
+
+        @pl.loop(0, 2)
+        def _(d):
+            finish(d, n - 1 - s)
+
+    pass_on(n - 2, True)
+
+    @pl.loop(0, 2)
+    def _(d):
+        finish(d, 1)
+
+    sib_p_copy().wait_send()
+
+    @pl.loop(0, n)
+    def _(q):
+        sib_b_copy(q).wait_send()
+
+    for d in range(2):
+        for u in range(SUB):
+            @pl.loop(0, n - 1)
+            def _(s):
+                red_copy(d, s, u).wait_send()
+                gat_copy(d, s, u, shard(d, s)).wait_send()
+
+            @pl.loop(0, n)
+            def _(t):
+                sib_a_copy(d, t, u, shard(d, t)).wait_send()
+
+
 def by_rows(factors, occupied_energy, virtual_energy, batch_orbitals, panel_order):
-    total = factors.shape[1]
+    n = lax.axis_size("pair")
+    depth, total = factors.shape
     batch_energy = batch_energies(occupied_energy, batch_orbitals)
-    nvir = virtual_energy.shape[0]
     energy = (virtual_energy[None, :] - batch_energy[:, None]).reshape(-1)
     panels = jnp.concatenate(
         [
@@ -108,21 +340,37 @@
             for k in range(panel_order.shape[0])
         ]
     )
-    partial = lax.dot_general(
-        panels,
-        factors,
-        (((0,), (0,)), ((), ())),
-        precision=lax.Precision.HIGH,
-        preferred_element_type=jnp.float32,
-    )
-    mine = lax.psum_scatter(partial, ("pair", "aux"), scatter_dimension=0, tiled=True)
-    rank = lax.axis_index("pair") * lax.axis_size("aux") + lax.axis_index("aux")
-    my_energy = lax.dynamic_slice_in_dim(chosen, rank * mine.shape[0], mine.shape[0], 0)
-    mine = os_scale * mine / (energy[None, :] + my_energy[:, None])
-    amplitudes = lax.all_gather(mine, ("pair", "aux"), axis=0, tiled=True)
-    return jnp.dot(
-        panels, amplitudes, precision=lax.Precision.HIGH, preferred_element_type=jnp.float32
-    )
+    window = panels.shape[1]
+    width = total // n
+    half, quarter = window // 2, window // 4
+    dma = pltpu.SemaphoreType.DMA
+    return pl.pallas_call(
+        functools.partial(ring_kernel, n),
+        out_shape=jax.ShapeDtypeStruct((depth, total), jnp.float32),
+        in_specs=[pl.BlockSpec(memory_space=pltpu.VMEM)] * 4,
+        out_specs=pl.BlockSpec(memory_space=pltpu.VMEM),
+        scratch_shapes=[
+            pltpu.VMEM((depth, total), jnp.float32),
+            pltpu.VMEM((depth, half), jnp.float32),
+            pltpu.VMEM((half, 2 * depth), jnp.bfloat16),
+            pltpu.VMEM((half, 2 * depth), jnp.bfloat16),
+            pltpu.VMEM((depth, window), jnp.bfloat16),
+            pltpu.VMEM((depth, window), jnp.bfloat16),
+            pltpu.VMEM((2, quarter, width), jnp.float32),
+            pltpu.VMEM((2, n, quarter, width), jnp.float32),
+            pltpu.VMEM((window, total), jnp.float32),
+            dma, dma, dma((n,)), dma((n,)),
+            dma((2, n - 1, SUB)), dma((2, n - 1, SUB)),
+            dma((2, n - 1, SUB)), dma((2, n - 1, SUB)),
+            dma((2, n, SUB)), dma((2, n, SUB)),
+        ],
+        compiler_params=pltpu.CompilerParams(
+            collective_id=0, has_side_effects=True, vmem_limit_bytes=48 * 1024 * 1024
+        ),
+        cost_estimate=pl.CostEstimate(
+            flops=12 * depth * window * total, bytes_accessed=8 * depth * total, transcendentals=0
+        ),
+    )(factors, panels, energy.reshape(1, total), chosen.reshape(window, 1))
 
 
 def on_device(factors, occupied_energy, virtual_energy, batch_orbitals, panel_order):

time: 229 us -> 116 us (0.51)
  waiting for transfers between devices: 180 us -> 0 us
  Pallas kernels: 0 us -> 91.3 us
  between operations: 24.3 us -> 10.7 us
  matrix products: 13.4 us -> 0 us
  local copies, waits for them, and re-layouts: 7.91 us -> 11.2 us
    reduce_scatter x1 -> x0, waiting for transfers between devices: 105 us -> none  [by_rows(): lax.psum_scatter(partial, ('pair', 'aux'), scatter_dimension=0, tiled=True)]
    pallas_call x0 -> x1, Pallas kernels: none -> 91.3 us  [by_rows(): pl.pallas_call(functools.partial(ring_kernel, n), out_shape=jax.ShapeDtyp...]
    all_gather x1 -> x0, waiting for transfers between devices: 75.2 us -> none  [by_rows(): amplitudes = lax.all_gather(mine, ('pair', 'aux'), axis=0, tiled=True)]
    dot_general x2 -> x0, matrix products: 13.4 us -> none  [the longest x1 7.56 us: by_rows(): jnp.dot(panels, amplitudes, precision=lax.Precision.HIGH, preferred_eleme...]
    unnamed x6 -> x5, local copies, waits for them, and re-layouts: 0.26 us -> 2.61 us
  transfers between devices with their start and end apart: 2 -> 0, of which waited for: 2 -> 0; matrix products, arithmetic and copies ran while one was open for 1% -> 0% of each run, Pallas kernels for 0% -> 0%
where the time goes in v1:
time: 116 us
  Pallas kernels  91.3 us (79%)
  local copies, waits for them, and re-layouts  11.2 us (10%)
  between operations  10.7 us (9%)
  other arithmetic  2.66 us (2%)
    pallas_call x1, Pallas kernels, by_rows(): pl.pallas_call(functools.partial(ring_kernel, n), out_shape=jax.ShapeDtyp...  91.3 us
    dynamic_slice x1, local copies, waits for them, and re-layouts, by_rows(): lax.dynamic_slice_in_dim(factors, panel_order[k] * PANEL, PANEL, 1)  3.41 us
    unnamed x5, local copies, waits for them, and re-layouts  2.61 us

profile of v1, /device:TPU:1, one launch (start us, length us, event | category | flops | bytes accessed | tf_op | source)
XLA Modules:
  0.0 115.9 jit_solution(5592154430834704762)
XLA Ops:
  0.7 1.3 %fusion = f32[]{:T(128)} fusion(f32[128]{0:T(128)} %param.6, s32[]{:T(128)} %bitcast.19), kind=kLoop, calls=%fused_computation.18 | loop fusion | flops 383 | bytes 520 | tf_op jit(solution)/shard_map/reduce_sum | solution.py:47
  2.0 1.3 %broadcast_subtract_fusion = f32[2048]{0:T(1024)S(1)} fusion(f32[2048]{0:T(1024)} %param.7, f32[]{:T(128)} %fusion), kind=kLoop, calls=%fused_computation | loop fusion | flops 2048 | bytes 16388 | tf_op jit(solution)/shard_map/sub | solution.py:329
  3.3 1.9 %fusion.2 = (s32[1]{0:T(128)}, s32[1]{0:T(128)}, s32[1]{0:T(128)}, s32[1]{0:T(128)}, s32[1]{0:T(128)}, /*index=5*/s32[1]{0:T(128)}, s32[1]{0:T(128)}, s32[1]{0:T...) fusion(s32[16]{0:T(128)} %param.9), kind=kLoop, calls=%fused_computation.20 | loop fusion | bytes 128 | tf_op jit(solution)/shard_map/slice | solution.py:332
  15.3 0.2 fusion.1
  15.4 0.1 concatenate.7
  15.5 1.0 copy.6.row_ref
  16.6 3.4 %constant_dynamic-slice_fusion = (f32[256,64]{1,0:T(8,128)S(1)}, f32[256,64]{1,0:T(8,128)S(1)}, f32[256,64]{1,0:T(8,128)S(1)}, f32[256,64]{1,0:T(8,128)}, f32[25...) fusion(f32[256,2048]{1,0:T(8,128)} %b_ref.1, ...), kind=kLoop, calls=%fused_computation.1 | loop fusion | bytes 2097216 | tf_op jit(solution)/shard_map/dynamic_slice | solution.py:332
  20.0 0.0 copy-start
  20.0 1.9 %concatenate.6.p_ref = f32[256,1024]{1,0:T(8,128)S(1)} concatenate(f32[256,64]{1,0:T(8,128)} %get-tuple-element.20, f32[256,64]{1,0:T(8,128)} %get-tuple-element.19, f32[256,64]{1,0:T(8,128)} %get-tuple-element.18, f32[256,64]{1,0:T(8,128)} %get-tuple-element.17, f32[256,64]{1,0:T(8,128)} %get-tuple-element.16, f32[256,64]{1,0:T(8,128)} %get-tuple-element.15, ...), dimensions={1} | concatenate | bytes 2097152 | tf_op jit(solution)/shard_map/concatenate | solution.py:330
  21.9 0.3 copy-done
  22.2 0.0 copy-start.1
  22.2 1.0 copy-done.1
  23.2 91.3 %shard_map.55 = f32[256,2048]{1,0:T(8,128)S(1)} custom-call(f32[256,2048]{1,0:T(8,128)S(1)} %copy-done, f32[256,1024]{1,0:T(8,128)S(1)} %concatenate.6.p_ref, f32[1,2048]{1,0:T(1,128)S(1)} %bitcast.20, f32[1024,1]{1,0:T(8,128)S(1)} %copy-done.1), custom_call_target="tpu_custom_call" | custom-call | flops 6442450944 | bytes 4194304 | tf_op jit(solution)/shard_map/pallas_call | solution.py:347
  114.5 1.3 %copy.9 = f32[256,2048]{1,0:T(8,128)} copy(f32[256,2048]{1,0:T(8,128)S(1)} %shard_map.55) | data formatting | bytes 4194304
Async XLA Ops:
  20.0 2.2 %copy-start = (f32[256,2048]{1,0:T(8,128)S(1)}, f32[256,2048]{1,0:T(8,128)}, u32[]{:S(2)}) copy-start(f32[256,2048]{1,0:T(8,128)} %b_ref.1) | copy-start | bytes 6291460
  22.2 1.0 copy-start.1

commit v2 on v1

--- a/solution.py
+++ b/solution.py
@@ -119,6 +119,34 @@
     return 2 * level + side
 
 
+def panel_pair(ref, first, second):
+    pair = 2 * PANEL
+
+    def load(number):
+        return ref[:, pl.ds(pl.multiple_of(number // 2 * pair, pair), pair)]
+
+    left, right = load(first), load(second)
+    left = jnp.where(first % 2 == 1, pltpu.roll(left, PANEL, 1), left)
+    right = jnp.where(second % 2 == 0, pltpu.roll(right, PANEL, 1), right)
+    lane = lax.broadcasted_iota(jnp.int32, left.shape, 1)
+    return jnp.where(lane < PANEL, left, right)
+
+
+def panel_kernel(
+    order_ref, batch_ref, occupied_ref, virtual_ref, b_ref, p_ref, col_ref, row_ref
+):
+    nvir = virtual_ref.shape[1]
+    for i in range(batch_ref.shape[0]):
+        col_ref[:, i * nvir : (i + 1) * nvir] = virtual_ref[...] - occupied_ref[batch_ref[i]]
+    pair = 2 * PANEL
+    for k in range(order_ref.shape[0] // 2):
+        first, second = order_ref[2 * k], order_ref[2 * k + 1]
+        here = slice(k * pair, (k + 1) * pair)
+        p_ref[:, here] = panel_pair(b_ref, first, second)
+        chosen = panel_pair(col_ref, first, second)
+        row_ref[here, :] = jnp.broadcast_to(chosen, (pair, pair)).T
+
+
 def ring_kernel(
     n, b_ref, p_ref, col_ref, row_ref, out_ref,
     sib_b, sib_p, pt_high, pt_low, p_high, p_low, part, buf, amp,
@@ -251,7 +279,7 @@
         for d in range(2):
             red_copy(d, n - 2, u).wait_recv()
             integrals = buf[d, n - 1, sub(u)] + part[d, sub(u)]
-            energy = col_ref[:, columns(place)] + row_ref[amp_rows(d, u), :]
+            energy = col_ref[:, columns(place)] + row_ref[amp_rows(d, u), 0:1]
             amp[amp_rows(d, u), columns(place)] = os_scale * integrals / energy
             gat_copy(d, 0, u, place).start()
             sib_a_copy(d, 0, u, place).start()
@@ -325,25 +353,21 @@
 def by_rows(factors, occupied_energy, virtual_energy, batch_orbitals, panel_order):
     n = lax.axis_size("pair")
     depth, total = factors.shape
-    batch_energy = batch_energies(occupied_energy, batch_orbitals)
-    energy = (virtual_energy[None, :] - batch_energy[:, None]).reshape(-1)
-    panels = jnp.concatenate(
-        [
-            lax.dynamic_slice_in_dim(factors, panel_order[k] * PANEL, PANEL, 1)
-            for k in range(panel_order.shape[0])
-        ],
-        axis=1,
-    )
-    chosen = jnp.concatenate(
-        [
-            lax.dynamic_slice_in_dim(energy, panel_order[k] * PANEL, PANEL, 0)
-            for k in range(panel_order.shape[0])
-        ]
-    )
-    window = panels.shape[1]
+    window = panel_order.shape[0] * PANEL
     width = total // n
     half, quarter = window // 2, window // 4
     dma = pltpu.SemaphoreType.DMA
+    panels, energy, chosen = pl.pallas_call(
+        panel_kernel,
+        out_shape=[
+            jax.ShapeDtypeStruct((depth, window), jnp.float32),
+            jax.ShapeDtypeStruct((1, total), jnp.float32),
+            jax.ShapeDtypeStruct((window, 2 * PANEL), jnp.float32),
+        ],
+        in_specs=[pl.BlockSpec(memory_space=pltpu.SMEM)] * 3
+        + [pl.BlockSpec(memory_space=pltpu.VMEM)] * 2,
+        out_specs=[pl.BlockSpec(memory_space=pltpu.VMEM)] * 3,
+    )(panel_order, batch_orbitals, occupied_energy, virtual_energy.reshape(1, -1), factors)
     return pl.pallas_call(
         functools.partial(ring_kernel, n),
         out_shape=jax.ShapeDtypeStruct((depth, total), jnp.float32),
@@ -370,7 +394,7 @@
         cost_estimate=pl.CostEstimate(
             flops=12 * depth * window * total, bytes_accessed=8 * depth * total, transcendentals=0
         ),
-    )(factors, panels, energy.reshape(1, total), chosen.reshape(window, 1))
+    )(factors, panels, energy, chosen)
 
 
 def on_device(factors, occupied_energy, virtual_energy, batch_orbitals, panel_order):

time: 116 us -> 100 us (0.86)
  between operations: 10.7 us -> 0.82 us
  local copies, waits for them, and re-layouts: 11.2 us -> 4.29 us
  Pallas kernels: 91.3 us -> 94.9 us
  other arithmetic: 2.66 us -> 0 us
    pallas_call x0 -> x1, Pallas kernels: none -> 3.58 us  [by_rows(): pl.pallas_call(panel_kernel, out_shape=[jax.ShapeDtypeStruct((depth, wind...]
    dynamic_slice x2 -> x0, local copies, waits for them, and re-layouts: 3.57 us -> none  [the longest x1 3.41 us: by_rows(): lax.dynamic_slice_in_dim(factors, panel_order[k] * PANEL, PANEL, 1)]
    concatenate x2 -> x0, local copies, waits for them, and re-layouts: 2.01 us -> none  [the longest x1 1.92 us: by_rows(): jnp.concatenate([lax.dynamic_slice_in_dim(factors, panel_order[k] * PANEL...]
    slice x1 -> x0, local copies, waits for them, and re-layouts: 1.94 us -> none  [by_rows(): panel_order[k] * PANEL]
    unnamed x5 -> x9, local copies, waits for them, and re-layouts: 2.61 us -> 4.29 us
    sub x1 -> x0, other arithmetic: 1.33 us -> none  [by_rows(): energy = (virtual_energy[None, :] - batch_energy[:, None]).reshape(-1)]
    reduce_sum x1 -> x0, other arithmetic: 1.33 us -> none  [batch_energies(): jnp.sum(jnp.where(batch_orbitals[:, None] == jnp.arange(noccupied, dtype=...]
where the time goes in v2:
time: 100 us
  Pallas kernels  94.9 us (95%)
  local copies, waits for them, and re-layouts  4.29 us (4%)
    pallas_call x1, Pallas kernels, by_rows(): pl.pallas_call(functools.partial(ring_kernel, n), out_shape=jax.ShapeDtyp...  91.3 us
    unnamed x9, local copies, waits for them, and re-layouts  4.29 us
    pallas_call x1, Pallas kernels, by_rows(): pl.pallas_call(panel_kernel, out_shape=[jax.ShapeDtypeStruct((depth, wind...  3.58 us

profile of v2, /device:TPU:1, one launch (start us, length us, event | category | flops | bytes accessed | tf_op | source)
XLA Modules:
  0.0 100.0 jit_solution(16075856753899830771)
XLA Ops:
  0.0 0.0 copy-start
  0.8 3.6 %shard_map.55 = (f32[256,1024]{1,0:T(8,128)}, f32[1,2048]{1,0:T(1,128)}, f32[1024,128]{1,0:T(8,128)}) custom-call(s32[16]{0:T(128)} %order_ref.1, s32[1]{0:T(128)S(6)} %copy.7.batch_ref, f32[128]{0:T(128)} %occupied_ref.1, f32[1,2048]{1,0:T(1,128)} %bitcast.1, f32[256,2048]{1,0:T(8,128)} %b_ref.3), custom_call_target="tpu_custom_call" | custom-call | tf_op jit(solution)/shard_map/pallas_call | solution.py:360
  4.4 0.0 copy-done
  4.4 0.0 copy-start.1
  4.4 1.2 %copy-done.1 = f32[256,1024]{1,0:T(8,128)S(1)} copy-done((f32[256,1024]{1,0:T(8,128)S(1)}, f32[256,1024]{1,0:T(8,128)}, u32[]{:S(2)}) %copy-start.1) | copy-done | bytes 1048600
  5.6 0.0 copy-start.2
  5.6 1.0 %copy-done.2 = f32[1024,128]{1,0:T(8,128)S(1)} copy-done((f32[1024,128]{1,0:T(8,128)S(1)}, f32[1024,128]{1,0:T(8,128)}, u32[]{:S(2)}) %copy-start.2) | copy-done | bytes 524312
  6.7 0.0 copy-start.3
  6.7 0.7 copy-done.3
  7.4 91.3 %shard_map.56 = f32[256,2048]{1,0:T(8,128)S(1)} custom-call(f32[256,2048]{1,0:T(8,128)S(1)} %copy-done, f32[256,1024]{1,0:T(8,128)S(1)} %copy-done.1, f32[1,2048]{1,0:T(1,128)S(1)} %copy-done.3, f32[1024,128]{1,0:T(8,128)S(1)} %copy-done.2), custom_call_target="tpu_custom_call" | custom-call | flops 6442450944 | bytes 4194304 | tf_op jit(solution)/shard_map/pallas_call | solution.py:371
  98.7 1.3 %copy.8 = f32[256,2048]{1,0:T(8,128)} copy(f32[256,2048]{1,0:T(8,128)S(1)} %shard_map.56) | data formatting | bytes 4194304
Async XLA Ops:
  0.0 4.4 %copy-start = (f32[256,2048]{1,0:T(8,128)S(1)}, f32[256,2048]{1,0:T(8,128)}, u32[]{:S(2)}) copy-start(f32[256,2048]{1,0:T(8,128)} %b_ref.3) | copy-start | bytes 6291460
  4.4 1.2 %copy-start.1 = (f32[256,1024]{1,0:T(8,128)S(1)}, f32[256,1024]{1,0:T(8,128)}, u32[]{:S(2)}) copy-start(f32[256,1024]{1,0:T(8,128)} %get-tuple-element.8.p_ref) | copy-start | bytes 3145732
  5.6 1.0 %copy-start.2 = (f32[1024,128]{1,0:T(8,128)S(1)}, f32[1024,128]{1,0:T(8,128)}, u32[]{:S(2)}) copy-start(f32[1024,128]{1,0:T(8,128)} %get-tuple-element.10.row_ref) | copy-start | bytes 1572868
  6.7 0.7 copy-start.3

commit v3 on v2

--- a/solution.py
+++ b/solution.py
@@ -132,33 +132,57 @@
     return jnp.where(lane < PANEL, left, right)
 
 
-def panel_kernel(
-    order_ref, batch_ref, occupied_ref, virtual_ref, b_ref, p_ref, col_ref, row_ref
+def sort_kernel(
+    order_ref, batch_ref, occupied_ref, virtual_ref, b_ref,
+    place_ref, b_out, col_out, row_out, source, energy,
 ):
     nvir = virtual_ref.shape[1]
     for i in range(batch_ref.shape[0]):
-        col_ref[:, i * nvir : (i + 1) * nvir] = virtual_ref[...] - occupied_ref[batch_ref[i]]
+        energy[:, i * nvir : (i + 1) * nvir] = virtual_ref[...] - occupied_ref[batch_ref[i]]
+    listed, panels = order_ref.shape[0], place_ref.shape[0]
+    for j in range(panels):
+        place_ref[j] = -1
+    for k in range(listed):
+        place_ref[order_ref[k]] = k
+        source[k] = order_ref[k]
+    free = jnp.int32(listed)
+    for j in range(panels):
+        found = place_ref[j]
+        source[free] = j
+        place_ref[j] = jnp.where(found < 0, free, found)
+        free = jnp.where(found < 0, free + 1, free)
     pair = 2 * PANEL
-    for k in range(order_ref.shape[0] // 2):
-        first, second = order_ref[2 * k], order_ref[2 * k + 1]
+    window = listed * PANEL
+    for k in range(panels // 2):
+        first, second = source[2 * k], source[2 * k + 1]
         here = slice(k * pair, (k + 1) * pair)
-        p_ref[:, here] = panel_pair(b_ref, first, second)
-        chosen = panel_pair(col_ref, first, second)
-        row_ref[here, :] = jnp.broadcast_to(chosen, (pair, pair)).T
+        b_out[:, here] = panel_pair(b_ref, first, second)
+        chosen = panel_pair(energy, first, second)
+        col_out[:, here] = chosen
+        if k < listed // 2:
+            row_out[here, :] = jnp.broadcast_to(chosen, (pair, pair)).T
+    row_out[window:, :] = row_out[: row_out.shape[0] - window, :]
+
+
+def unsort_kernel(place_ref, d_ref, out_ref):
+    pair = 2 * PANEL
+    for k in range(place_ref.shape[0] // 2):
+        here = slice(k * pair, (k + 1) * pair)
+        out_ref[:, here] = panel_pair(d_ref, place_ref[2 * k], place_ref[2 * k + 1])
 
 
 def ring_kernel(
-    n, b_ref, p_ref, col_ref, row_ref, out_ref,
-    sib_b, sib_p, pt_high, pt_low, p_high, p_low, part, buf, amp,
+    n, b_ref, col_ref, row_ref, out_ref,
+    sib_b, pt_high, pt_low, p_high, p_low, energy, part, buf, amp,
     sibp_send, sibp_recv, sibb_send, sibb_recv,
     red_send, red_recv, gat_send, gat_recv, siba_send, siba_recv,
 ):
     depth, total = b_ref.shape
-    window = p_ref.shape[1]
-    width = total // n
-    half = window // 2
-    quarter = half // 2
-    rows = quarter // SUB
+    window = total // 2
+    width = window // n
+    near = (n // 2 + 1) * width
+    near_rows, far_rows = near // 4, window // 4
+    rows = (near_rows + far_rows) // SUB
     core = lax.axis_index("aux")
     place = ring_place(lax.axis_index("pair"), n)
 
@@ -170,25 +194,31 @@
     def columns(q):
         return pl.ds(pl.multiple_of(q * width, width), width)
 
+    def far_columns(q):
+        return pl.ds(pl.multiple_of(window + q * width, width), width)
+
+    def near_span(d, q):
+        return pl.ds(pl.multiple_of(q * width + (2 * core + d) * near_rows, 32), near_rows)
+
+    def far_span(d):
+        return pl.ds(pl.multiple_of((2 * core + d) * far_rows, 32), far_rows)
+
     def shard(d, step):
         return (place + n * n + (2 * d - 1) * step) % n
 
     def sib_p_copy():
         return pltpu.make_async_remote_copy(
-            p_ref.at[:, pl.ds(pl.multiple_of((1 - core) * half, half), half)], sib_p,
+            b_ref.at[:, pl.ds(0, window)], sib_b.at[:, pl.ds(0, window)],
             sibp_send, sibp_recv, device_id=sibling, device_id_type=pl.DeviceIdType.MESH)
 
     def sib_b_copy(q):
         return pltpu.make_async_remote_copy(
-            b_ref.at[:, columns(q)], sib_b.at[:, columns(q)],
+            b_ref.at[:, far_columns(q)], sib_b.at[:, far_columns(q)],
             sibb_send.at[q], sibb_recv.at[q], device_id=sibling,
             device_id_type=pl.DeviceIdType.MESH)
 
     def sub(u):
         return pl.ds(pl.multiple_of(u * rows, rows), rows)
-
-    def amp_rows(d, u):
-        return pl.ds(pl.multiple_of(core * half + d * quarter + u * rows, rows), rows)
 
     def red_copy(d, s, u):
         return pltpu.make_async_remote_copy(
@@ -197,21 +227,19 @@
             device_id_type=pl.DeviceIdType.MESH)
 
     def gat_copy(d, s, u, q):
-        block = amp.at[amp_rows(d, u), columns(q)]
+        block = amp.at[q, core, d, sub(u)]
         return pltpu.make_async_remote_copy(
             block, block, gat_send.at[d, s, u], gat_recv.at[d, s, u],
             device_id=neighbour(d), device_id_type=pl.DeviceIdType.MESH)
 
     def sib_a_copy(d, t, u, q):
-        block = amp.at[amp_rows(d, u), columns(q)]
+        block = amp.at[q, core, d, sub(u)]
         return pltpu.make_async_remote_copy(
             block, block, siba_send.at[d, t, u], siba_recv.at[d, t, u],
             device_id=sibling, device_id_type=pl.DeviceIdType.MESH)
 
     def sib_a_arrival(d, t, u, q):
-        block = amp.at[
-            pl.ds(pl.multiple_of((1 - core) * half + d * quarter + u * rows, rows), rows),
-            columns(q)]
+        block = amp.at[q, 1 - core, d, sub(u)]
         return pltpu.make_async_remote_copy(
             block, block, siba_send.at[d, t, u], siba_recv.at[d, t, u],
             device_id=sibling, device_id_type=pl.DeviceIdType.MESH)
@@ -228,21 +256,24 @@
             sib_b_copy(shard(1, i)).start()
     sib_b_copy(place).start()
 
-    mine = pl.ds(pl.multiple_of(core * half, half), half)
-    high, low = split(p_ref[:, mine].T)
-    pt_high[:, :depth] = high
-    pt_low[:, :depth] = low
+    def set_transposed(ref, span):
+        high, low = split(ref[:, :window].T)
+        pt_high[:window, span] = high
+        pt_low[:window, span] = low
+        pt_high[window:, span] = high[:near]
+        pt_low[window:, span] = low[:near]
+
+    set_transposed(b_ref, slice(0, depth))
     sib_p_copy().wait_recv()
-    high, low = split(sib_p[...].T)
-    pt_high[:, depth:] = high
-    pt_low[:, depth:] = low
+    set_transposed(sib_b, slice(depth, 2 * depth))
 
     def set_part(d, q):
-        lhs = pl.ds(pl.multiple_of(d * quarter, quarter), quarter)
-        own_high, own_low = split(b_ref[:, columns(q)])
-        sib_high, sib_low = split(sib_b[:, columns(q)])
-        part[d] = dot3(pt_high[lhs, :depth], pt_low[lhs, :depth], own_high, own_low) + dot3(
-            pt_high[lhs, depth:], pt_low[lhs, depth:], sib_high, sib_low)
+        def product(lhs, cols):
+            both = jnp.concatenate([b_ref[:, cols], sib_b[:, cols]], axis=0)
+            return dot3(pt_high[lhs, :], pt_low[lhs, :], *split(both))
+
+        part[d, :near_rows] = product(near_span(d, q), columns(q))
+        part[d, near_rows:] = product(far_span(d), far_columns(q))
 
     @pl.loop(0, 2)
     def _(d):
@@ -257,9 +288,15 @@
         if i < n // 2:
             sib_b_copy(shard(1, i)).wait_recv()
     sib_b_copy(place).wait_recv()
-    high, low = split(p_ref[...])
-    p_high[...] = high
-    p_low[...] = low
+    high, low = split(b_ref[:, :window])
+    p_high[:, :window] = high
+    p_low[:, :window] = low
+    p_high[:, window:] = high[:, :near]
+    p_low[:, window:] = low[:, :near]
+    out_ref[:, :window] = jnp.zeros((depth, window), jnp.float32)
+    for d in range(2):
+        energy[d, :near_rows] = row_ref[near_span(d, place), :] + col_ref[:, columns(place)]
+        energy[d, near_rows:] = row_ref[far_span(d), :] + col_ref[:, far_columns(place)]
 
     @pl.loop(1, n - 1)
     def _(s):
@@ -279,8 +316,7 @@
         for d in range(2):
             red_copy(d, n - 2, u).wait_recv()
             integrals = buf[d, n - 1, sub(u)] + part[d, sub(u)]
-            energy = col_ref[:, columns(place)] + row_ref[amp_rows(d, u), 0:1]
-            amp[amp_rows(d, u), columns(place)] = os_scale * integrals / energy
+            amp[place, core, d, sub(u)] = os_scale * integrals / energy[d, sub(u)]
             gat_copy(d, 0, u, place).start()
             sib_a_copy(d, 0, u, place).start()
 
@@ -294,12 +330,21 @@
                 sib_a_copy(d, s + 1, u, q).start()
 
     def density(q):
-        total_sum = jnp.zeros((depth, width), jnp.float32)
-        for k in range(4):
-            span = pl.ds(k * quarter, quarter)
-            a_high, a_low = split(amp[span, columns(q)])
-            total_sum += dot3(p_high[:, span], p_low[:, span], a_high, a_low)
-        out_ref[:, columns(q)] = total_sum
+        far = jnp.zeros((depth, width), jnp.float32)
+        for j in range(4):
+            span = slice(j * far_rows, (j + 1) * far_rows)
+            far += dot3(
+                p_high[:, span], p_low[:, span], *split(amp[q, j // 2, j % 2, near_rows:]))
+        out_ref[:, far_columns(q)] = far
+        block = jnp.concatenate([amp[q, j // 2, j % 2, :near_rows] for j in range(4)], axis=0)
+        high, low = split(block)
+        span = pl.ds(pl.multiple_of(q * width, width), near)
+        out_ref[:, columns(q)] += dot3(p_high[:, span], p_low[:, span], high, low)
+        q_high, q_low = p_high[:, columns(q)], p_low[:, columns(q)]
+        for i in range(1, n // 2):
+            there = slice(i * width, (i + 1) * width)
+            out_ref[:, columns((q + i) % n)] += dot3(
+                q_high, q_low, high[there].T, low[there].T)
 
     def finish(d, j):
         q = shard(d, j)
@@ -354,35 +399,41 @@
     n = lax.axis_size("pair")
     depth, total = factors.shape
     window = panel_order.shape[0] * PANEL
-    width = total // n
-    half, quarter = window // 2, window // 4
+    width = window // n
+    near = (n // 2 + 1) * width
+    stream = (near + window) // 4
     dma = pltpu.SemaphoreType.DMA
-    panels, energy, chosen = pl.pallas_call(
-        panel_kernel,
+    smem, vmem = pl.BlockSpec(memory_space=pltpu.SMEM), pl.BlockSpec(memory_space=pltpu.VMEM)
+    place, ordered, energy, rows = pl.pallas_call(
+        sort_kernel,
         out_shape=[
-            jax.ShapeDtypeStruct((depth, window), jnp.float32),
+            jax.ShapeDtypeStruct((total // PANEL,), jnp.int32),
+            jax.ShapeDtypeStruct((depth, total), jnp.float32),
             jax.ShapeDtypeStruct((1, total), jnp.float32),
-            jax.ShapeDtypeStruct((window, 2 * PANEL), jnp.float32),
+            jax.ShapeDtypeStruct((window + near, 2 * PANEL), jnp.float32),
         ],
-        in_specs=[pl.BlockSpec(memory_space=pltpu.SMEM)] * 3
-        + [pl.BlockSpec(memory_space=pltpu.VMEM)] * 2,
-        out_specs=[pl.BlockSpec(memory_space=pltpu.VMEM)] * 3,
+        in_specs=[smem] * 3 + [vmem] * 2,
+        out_specs=[smem] + [vmem] * 3,
+        scratch_shapes=[
+            pltpu.SMEM((total // PANEL + 1,), jnp.int32),
+            pltpu.VMEM((1, total), jnp.float32),
+        ],
     )(panel_order, batch_orbitals, occupied_energy, virtual_energy.reshape(1, -1), factors)
-    return pl.pallas_call(
+    density = pl.pallas_call(
         functools.partial(ring_kernel, n),
         out_shape=jax.ShapeDtypeStruct((depth, total), jnp.float32),
-        in_specs=[pl.BlockSpec(memory_space=pltpu.VMEM)] * 4,
-        out_specs=pl.BlockSpec(memory_space=pltpu.VMEM),
+        in_specs=[vmem] * 3,
+        out_specs=vmem,
         scratch_shapes=[
             pltpu.VMEM((depth, total), jnp.float32),
-            pltpu.VMEM((depth, half), jnp.float32),
-            pltpu.VMEM((half, 2 * depth), jnp.bfloat16),
-            pltpu.VMEM((half, 2 * depth), jnp.bfloat16),
-            pltpu.VMEM((depth, window), jnp.bfloat16),
-            pltpu.VMEM((depth, window), jnp.bfloat16),
-            pltpu.VMEM((2, quarter, width), jnp.float32),
-            pltpu.VMEM((2, n, quarter, width), jnp.float32),
-            pltpu.VMEM((window, total), jnp.float32),
+            pltpu.VMEM((window + near, 2 * depth), jnp.bfloat16),
+            pltpu.VMEM((window + near, 2 * depth), jnp.bfloat16),
+            pltpu.VMEM((depth, window + near), jnp.bfloat16),
+            pltpu.VMEM((depth, window + near), jnp.bfloat16),
+            pltpu.VMEM((2, stream, width), jnp.float32),
+            pltpu.VMEM((2, stream, width), jnp.float32),
+            pltpu.VMEM((2, n, stream, width), jnp.float32),
+            pltpu.VMEM((n, 2, 2, stream, width), jnp.float32),
             dma, dma, dma((n,)), dma((n,)),
             dma((2, n - 1, SUB)), dma((2, n - 1, SUB)),
             dma((2, n - 1, SUB)), dma((2, n - 1, SUB)),
@@ -394,12 +445,19 @@
         cost_estimate=pl.CostEstimate(
             flops=12 * depth * window * total, bytes_accessed=8 * depth * total, transcendentals=0
         ),
-    )(factors, panels, energy, chosen)
+    )(ordered, energy, rows)
+    return pl.pallas_call(
+        unsort_kernel,
+        out_shape=jax.ShapeDtypeStruct((depth, total), jnp.float32),
+        in_specs=[smem, vmem],
+        out_specs=vmem,
+    )(place, density)
 
 
 def on_device(factors, occupied_energy, virtual_energy, batch_orbitals, panel_order):
     window = panel_order.shape[0] * PANEL
-    fits = 4 * window * factors.shape[1] <= 8 * 1024 * 1024
+    n = lax.axis_size("pair")
+    fits = n % 2 == 0 and window == 2 * PANEL * n and factors.shape[1] == 2 * window
     plan = by_rows if fits else by_columns
     return plan(factors, occupied_energy, virtual_energy, batch_orbitals, panel_order)
 

time: 100 us -> 96.1 us (0.961)
  Pallas kernels: 94.9 us -> 90.4 us
    pallas_call x1, Pallas kernels: 91.3 us -> 81.4 us  [by_rows(): pl.pallas_call(functools.partial(ring_kernel, n), out_shape=jax.ShapeDtyp...]
    pallas_call x1 -> x2, Pallas kernels: 3.58 us -> 8.93 us  [the longest x1 4.83 us: by_rows(): pl.pallas_call(sort_kernel, out_shape=[jax.ShapeDtypeStruct((total // PAN...]
    unnamed x9 -> x8, local copies, waits for them, and re-layouts: 4.29 us -> 4.76 us
where the time goes in v3:
time: 96.1 us; the launch traced here: 95.8 us
  Pallas kernels  90.4 us (94%)
  local copies, waits for them, and re-layouts  4.76 us (5%)
    pallas_call x1, Pallas kernels, by_rows(): pl.pallas_call(functools.partial(ring_kernel, n), out_shape=jax.ShapeDtyp...  81.4 us
    pallas_call x1, Pallas kernels, by_rows(): pl.pallas_call(sort_kernel, out_shape=[jax.ShapeDtypeStruct((total // PAN...  4.83 us
    unnamed x8, local copies, waits for them, and re-layouts  4.76 us
    pallas_call x1, Pallas kernels, by_rows(): pl.pallas_call(unsort_kernel, out_shape=jax.ShapeDtypeStruct((depth, tota...  4.1 us

profile of v3, /device:TPU:1, one launch (start us, length us, event | category | flops | bytes accessed | tf_op | source)
XLA Modules:
  0.0 95.8 jit_solution(12705311563522994520)
XLA Ops:
  0.7 4.8 %shard_map.55 = (s32[32]{0:T(128)}, f32[256,2048]{1,0:T(8,128)}, f32[1,2048]{1,0:T(1,128)}, f32[1664,128]{1,0:T(8,128)}) custom-call(s32[16]{0:T(128)} %order_ref.1, s32[1]{0:T(128)S(6)} %copy.6.batch_ref, f32[128]{0:T(128)} %occupied_ref.1, f32[1,2048]{1,0:T(1,128)} %bitcast.1, f32[256,2048]{1,0:T(8,128)} %b_ref.1), custom_call_target="tpu_custom_call" | custom-call | tf_op jit(solution)/shard_map/pallas_call | solution.py:407
  5.5 0.0 copy-start.1
  5.5 1.6 %copy-done.1 = f32[256,2048]{1,0:T(8,128)S(1)} copy-done((f32[256,2048]{1,0:T(8,128)S(1)}, f32[256,2048]{1,0:T(8,128)}, u32[]{:S(2)}) %copy-start.1) | copy-done | bytes 2097176
  7.1 0.0 copy-start.2
  7.1 1.2 %copy-done.2 = f32[1664,128]{1,0:T(8,128)S(1)} copy-done((f32[1664,128]{1,0:T(8,128)S(1)}, f32[1664,128]{1,0:T(8,128)}, u32[]{:S(2)}) %copy-start.2) | copy-done | bytes 851992
  8.2 0.0 copy-start.3
  8.2 0.7 copy-done.3
  8.9 81.4 %shard_map.56.d_ref = f32[256,2048]{1,0:T(8,128)S(1)} custom-call(f32[256,2048]{1,0:T(8,128)S(1)} %copy-done.1, f32[1,2048]{1,0:T(1,128)S(1)} %copy-done.3, f32[1664,128]{1,0:T(8,128)S(1)} %copy-done.2), custom_call_target="tpu_custom_call" | custom-call | flops 6442450944 | bytes 4194304 | tf_op jit(solution)/shard_map/pallas_call | solution.py:422
  90.4 0.0 copy-start
  90.4 1.3 %copy-done = f32[256,2048]{1,0:T(8,128)} copy-done((f32[256,2048]{1,0:T(8,128)}, f32[256,2048]{1,0:T(8,128)S(1)}, u32[]{:S(2)}) %copy-start) | copy-done | bytes 2097176
  91.7 4.1 %shard_map.57 = f32[256,2048]{1,0:T(8,128)} custom-call(s32[32]{0:T(128)} %get-tuple-element.9.place_ref, f32[256,2048]{1,0:T(8,128)} %copy-done), custom_call_target="tpu_custom_call" | custom-call | tf_op jit(solution)/shard_map/pallas_call | solution.py:449
Async XLA Ops:
  5.5 1.6 %copy-start.1 = (f32[256,2048]{1,0:T(8,128)S(1)}, f32[256,2048]{1,0:T(8,128)}, u32[]{:S(2)}) copy-start(f32[256,2048]{1,0:T(8,128)} %get-tuple-element.10.b_ref) | copy-start | bytes 6291460
  7.1 1.2 %copy-start.2 = (f32[1664,128]{1,0:T(8,128)S(1)}, f32[1664,128]{1,0:T(8,128)}, u32[]{:S(2)}) copy-start(f32[1664,128]{1,0:T(8,128)} %get-tuple-element.12.row_ref) | copy-start | bytes 2555908
  8.2 0.7 copy-start.3
  90.4 1.3 %copy-start = (f32[256,2048]{1,0:T(8,128)}, f32[256,2048]{1,0:T(8,128)S(1)}, u32[]{:S(2)}) copy-start(f32[256,2048]{1,0:T(8,128)S(1)} %shard_map.56.d_ref) | copy-start | bytes 6291460

commit v4 on v3

--- a/solution.py
+++ b/solution.py
@@ -134,8 +134,9 @@
 
 def sort_kernel(
     order_ref, batch_ref, occupied_ref, virtual_ref, b_ref,
-    place_ref, b_out, col_out, row_out, source, energy,
+    place_ref, b_out, source, energy,
 ):
+    depth = b_ref.shape[0]
     nvir = virtual_ref.shape[1]
     for i in range(batch_ref.shape[0]):
         energy[:, i * nvir : (i + 1) * nvir] = virtual_ref[...] - occupied_ref[batch_ref[i]]
@@ -152,16 +153,11 @@
         place_ref[j] = jnp.where(found < 0, free, found)
         free = jnp.where(found < 0, free + 1, free)
     pair = 2 * PANEL
-    window = listed * PANEL
     for k in range(panels // 2):
         first, second = source[2 * k], source[2 * k + 1]
         here = slice(k * pair, (k + 1) * pair)
-        b_out[:, here] = panel_pair(b_ref, first, second)
-        chosen = panel_pair(energy, first, second)
-        col_out[:, here] = chosen
-        if k < listed // 2:
-            row_out[here, :] = jnp.broadcast_to(chosen, (pair, pair)).T
-    row_out[window:, :] = row_out[: row_out.shape[0] - window, :]
+        b_out[:depth, here] = panel_pair(b_ref, first, second)
+        b_out[depth:, here] = jnp.broadcast_to(panel_pair(energy, first, second), (8, pair))
 
 
 def unsort_kernel(place_ref, d_ref, out_ref):
@@ -172,12 +168,12 @@
 
 
 def ring_kernel(
-    n, b_ref, col_ref, row_ref, out_ref,
-    sib_b, pt_high, pt_low, p_high, p_low, energy, part, buf, amp,
+    n, b_ref, out_ref,
+    row_ref, sib_b, pt_high, pt_low, p_high, p_low, energy, part, buf, amp,
     sibp_send, sibp_recv, sibb_send, sibb_recv,
     red_send, red_recv, gat_send, gat_recv, siba_send, siba_recv,
 ):
-    depth, total = b_ref.shape
+    depth, total = out_ref.shape
     window = total // 2
     width = window // n
     near = (n // 2 + 1) * width
@@ -208,12 +204,12 @@
 
     def sib_p_copy():
         return pltpu.make_async_remote_copy(
-            b_ref.at[:, pl.ds(0, window)], sib_b.at[:, pl.ds(0, window)],
+            b_ref.at[pl.ds(0, depth), pl.ds(0, window)], sib_b.at[:, pl.ds(0, window)],
             sibp_send, sibp_recv, device_id=sibling, device_id_type=pl.DeviceIdType.MESH)
 
     def sib_b_copy(q):
         return pltpu.make_async_remote_copy(
-            b_ref.at[:, far_columns(q)], sib_b.at[:, far_columns(q)],
+            b_ref.at[pl.ds(0, depth), far_columns(q)], sib_b.at[:, far_columns(q)],
             sibb_send.at[q], sibb_recv.at[q], device_id=sibling,
             device_id_type=pl.DeviceIdType.MESH)
 
@@ -257,7 +253,7 @@
     sib_b_copy(place).start()
 
     def set_transposed(ref, span):
-        high, low = split(ref[:, :window].T)
+        high, low = split(ref[:depth, :window].T)
         pt_high[:window, span] = high
         pt_low[:window, span] = low
         pt_high[window:, span] = high[:near]
@@ -269,7 +265,7 @@
 
     def set_part(d, q):
         def product(lhs, cols):
-            both = jnp.concatenate([b_ref[:, cols], sib_b[:, cols]], axis=0)
+            both = jnp.concatenate([b_ref[:depth, cols], sib_b[:, cols]], axis=0)
             return dot3(pt_high[lhs, :], pt_low[lhs, :], *split(both))
 
         part[d, :near_rows] = product(near_span(d, q), columns(q))
@@ -288,15 +284,22 @@
         if i < n // 2:
             sib_b_copy(shard(1, i)).wait_recv()
     sib_b_copy(place).wait_recv()
-    high, low = split(b_ref[:, :window])
+    high, low = split(b_ref[:depth, :window])
     p_high[:, :window] = high
     p_low[:, :window] = low
     p_high[:, window:] = high[:, :near]
     p_low[:, window:] = low[:, :near]
     out_ref[:, :window] = jnp.zeros((depth, window), jnp.float32)
+    for k in range(n):
+        here = slice(k * width, (k + 1) * width)
+        one = b_ref[depth : depth + 1, here]
+        row_ref[here, :] = jnp.broadcast_to(one, (width, width)).T
+    row_ref[window:, :] = row_ref[:near, :]
     for d in range(2):
-        energy[d, :near_rows] = row_ref[near_span(d, place), :] + col_ref[:, columns(place)]
-        energy[d, near_rows:] = row_ref[far_span(d), :] + col_ref[:, far_columns(place)]
+        near_energy = b_ref[depth : depth + 1, columns(place)]
+        far_energy = b_ref[depth : depth + 1, far_columns(place)]
+        energy[d, :near_rows] = row_ref[near_span(d, place), :] + near_energy
+        energy[d, near_rows:] = row_ref[far_span(d), :] + far_energy
 
     @pl.loop(1, n - 1)
     def _(s):
@@ -319,15 +322,6 @@
             amp[place, core, d, sub(u)] = os_scale * integrals / energy[d, sub(u)]
             gat_copy(d, 0, u, place).start()
             sib_a_copy(d, 0, u, place).start()
-
-    def pass_on(s, last):
-        for u in range(SUB):
-            for d in range(2):
-                q = shard(d, s + 1)
-                gat_copy(d, s, u, q).wait_recv()
-                if not last:
-                    gat_copy(d, s + 1, u, q).start()
-                sib_a_copy(d, s + 1, u, q).start()
 
     def density(q):
         far = jnp.zeros((depth, width), jnp.float32)
@@ -355,23 +349,27 @@
 
     middle = n // 2
 
-    @pl.loop(0, middle)
+    @pl.loop(0, n - 1)
     def _(s):
-        pass_on(s, False)
-
-    @pl.loop(0, 2)
-    def _(i):
-        finish(0, i * middle)
-
-    @pl.loop(middle, n - 2)
-    def _(s):
-        pass_on(s, False)
-
-        @pl.loop(0, 2)
-        def _(d):
-            finish(d, n - 1 - s)
-
-    pass_on(n - 2, True)
+        for u in range(SUB):
+            for d in range(2):
+                q = shard(d, s + 1)
+                gat_copy(d, s, u, q).wait_recv()
+
+                @pl.when(s < n - 2)
+                def _():
+                    gat_copy(d, s + 1, u, q).start()
+
+                sib_a_copy(d, s + 1, u, q).start()
+
+            if u == 0:
+                @pl.when((s == 1) | (s >= middle))
+                def _():
+                    finish(0, (n - s) % (n - 1))
+            elif u == SUB // 2:
+                @pl.when(s > middle)
+                def _():
+                    finish(1, n - s)
 
     @pl.loop(0, 2)
     def _(d):
@@ -404,16 +402,14 @@
     stream = (near + window) // 4
     dma = pltpu.SemaphoreType.DMA
     smem, vmem = pl.BlockSpec(memory_space=pltpu.SMEM), pl.BlockSpec(memory_space=pltpu.VMEM)
-    place, ordered, energy, rows = pl.pallas_call(
+    place, ordered = pl.pallas_call(
         sort_kernel,
         out_shape=[
             jax.ShapeDtypeStruct((total // PANEL,), jnp.int32),
-            jax.ShapeDtypeStruct((depth, total), jnp.float32),
-            jax.ShapeDtypeStruct((1, total), jnp.float32),
-            jax.ShapeDtypeStruct((window + near, 2 * PANEL), jnp.float32),
+            jax.ShapeDtypeStruct((depth + 8, total), jnp.float32),
         ],
         in_specs=[smem] * 3 + [vmem] * 2,
-        out_specs=[smem] + [vmem] * 3,
+        out_specs=[smem, vmem],
         scratch_shapes=[
             pltpu.SMEM((total // PANEL + 1,), jnp.int32),
             pltpu.VMEM((1, total), jnp.float32),
@@ -422,9 +418,10 @@
     density = pl.pallas_call(
         functools.partial(ring_kernel, n),
         out_shape=jax.ShapeDtypeStruct((depth, total), jnp.float32),
-        in_specs=[vmem] * 3,
+        in_specs=[vmem],
         out_specs=vmem,
         scratch_shapes=[
+            pltpu.VMEM((window + near, width), jnp.float32),
             pltpu.VMEM((depth, total), jnp.float32),
             pltpu.VMEM((window + near, 2 * depth), jnp.bfloat16),
             pltpu.VMEM((window + near, 2 * depth), jnp.bfloat16),
@@ -445,12 +442,13 @@
         cost_estimate=pl.CostEstimate(
             flops=12 * depth * window * total, bytes_accessed=8 * depth * total, transcendentals=0
         ),
-    )(ordered, energy, rows)
+    )(ordered)
     return pl.pallas_call(
         unsort_kernel,
         out_shape=jax.ShapeDtypeStruct((depth, total), jnp.float32),
-        in_specs=[smem, vmem],
-        out_specs=vmem,
+        grid=(4,),
+        in_specs=[smem, pl.BlockSpec((depth // 4, total), lambda i: (i, 0))],
+        out_specs=pl.BlockSpec((depth // 4, total), lambda i: (i, 0)),
     )(place, density)
 
 

time: 96.1 us -> 93.3 us (0.971)
  local copies, waits for them, and re-layouts: 4.76 us -> 2.93 us
  Pallas kernels: 90.4 us -> 89.2 us
    unnamed x8 -> x4, local copies, waits for them, and re-layouts: 4.76 us -> 2.93 us
where the time goes in v4:
time: 93.3 us; the launch traced here: 92.9 us
  Pallas kernels  89.2 us (96%)
  local copies, waits for them, and re-layouts  2.93 us (3%)
    pallas_call x1, Pallas kernels, by_rows(): pl.pallas_call(functools.partial(ring_kernel, n), out_shape=jax.ShapeDtyp...  80.5 us
    pallas_call x1, Pallas kernels, by_rows(): pl.pallas_call(unsort_kernel, out_shape=jax.ShapeDtypeStruct((depth, tota...  4.42 us
    pallas_call x1, Pallas kernels, by_rows(): pl.pallas_call(sort_kernel, out_shape=[jax.ShapeDtypeStruct((total // PAN...  4.33 us
    unnamed x4, local copies, waits for them, and re-layouts  2.93 us

profile of v4, /device:TPU:1, one launch (start us, length us, event | category | flops | bytes accessed | tf_op | source)
XLA Modules:
  0.0 92.9 jit_solution(4466656806371255786)
XLA Ops:
  0.7 4.3 %shard_map.55 = (s32[32]{0:T(128)}, f32[264,2048]{1,0:T(8,128)}) custom-call(s32[16]{0:T(128)} %order_ref.1, s32[1]{0:T(128)S(6)} %copy.6.batch_ref, f32[128]{0:T(128)} %occupied_ref.1, f32[1,2048]{1,0:T(1,128)} %bitcast.1, f32[256,2048]{1,0:T(8,128)} %b_ref.1), custom_call_target="tpu_custom_call" | custom-call | tf_op jit(solution)/shard_map/pallas_call | solution.py:405
  5.0 0.0 copy-start.1
  5.0 1.6 %copy-done.1 = f32[264,2048]{1,0:T(8,128)S(1)} copy-done((f32[264,2048]{1,0:T(8,128)S(1)}, f32[264,2048]{1,0:T(8,128)}, u32[]{:S(2)}) %copy-start.1) | copy-done | bytes 2162712
  6.6 80.5 %shard_map.56.d_ref = f32[256,2048]{1,0:T(8,128)S(1)} custom-call(f32[264,2048]{1,0:T(8,128)S(1)} %copy-done.1), custom_call_target="tpu_custom_call" | custom-call | flops 6442450944 | bytes 4194304 | tf_op jit(solution)/shard_map/pallas_call | solution.py:418
  87.1 0.0 copy-start
  87.1 1.3 %copy-done = f32[256,2048]{1,0:T(8,128)} copy-done((f32[256,2048]{1,0:T(8,128)}, f32[256,2048]{1,0:T(8,128)S(1)}, u32[]{:S(2)}) %copy-start) | copy-done | bytes 2097176
  88.4 4.4 %shard_map.57 = f32[256,2048]{1,0:T(8,128)} custom-call(s32[32]{0:T(128)} %get-tuple-element.7.place_ref, f32[256,2048]{1,0:T(8,128)} %copy-done), custom_call_target="tpu_custom_call" | custom-call | tf_op jit(solution)/shard_map/pallas_call | solution.py:446
Async XLA Ops:
  5.0 1.6 %copy-start.1 = (f32[264,2048]{1,0:T(8,128)S(1)}, f32[264,2048]{1,0:T(8,128)}, u32[]{:S(2)}) copy-start(f32[264,2048]{1,0:T(8,128)} %get-tuple-element.8.b_ref) | copy-start | bytes 6488068
  87.1 1.3 %copy-start = (f32[256,2048]{1,0:T(8,128)}, f32[256,2048]{1,0:T(8,128)S(1)}, u32[]{:S(2)}) copy-start(f32[256,2048]{1,0:T(8,128)S(1)} %shard_map.56.d_ref) | copy-start | bytes 6291460
